TPU v7x, 256 devices: a whole 4x4x8 slice. The times are simulated.
256 devices in a mesh: blk: 64 (over y, z, x_hi), rep: 4 (over x_lo, core).
Axes of the slice: x: 4 (x_hi: 2, x_lo: 2; x = x_hi * 2 + x_lo), y: 4, z: 8, core: 2. Of those that a mesh axis runs over, the one named last changes fastest.
Arguments:
- embeddings: bfloat16 [131072, 256], P('blk'), may hold values from -6 to 6
- counts: int32 [64], P('blk'), may hold values from 128 to 2048, as said below
- validity: int32 [131072], P('blk'), may hold values 0 or 1
Outputs:
- log_density: float32 [131072], P('blk')
- mean_embedding: float32 [131072, 256], P('blk', 'rep')
Inputs may be any that keep to these rules, and one draw needn't show every extreme that they name: `counts`: every count is a multiple of 128, and some block is full.
All inputs are finite; a program needn't handle non-finite values. No bound on the sum of `validity` on one device may be relied on, other than what follows from the above.
Results may differ from a plain program's by a relative error of at most 0.0047.
Values may be sent and summed in bfloat16 or wider, within the bound.
No kernel may reach another device: no remote copies, remote signals or barrier semaphores. Data moves between devices by JAX's collectives and lax.ppermute only.
A program may use at most 64 MiB of HBM per device.

v0:
```python
import functools
import math

import jax
import jax.numpy as jnp
from jax import lax
from jax.experimental import pallas as pl
from jax.experimental.pallas import tpu as pltpu
from jax.sharding import PartitionSpec as P

BETA = 8.0
EPSILON = 1e-06
LOG2E = math.log2(math.e)
DEAD = -1e30

SLOTS = 2048
WIDTH = 256
SHARE = 512
GRANULE = 128
EXTRA = 8
TILE = 512
PART = 64
PIECES = (1280, 768)

F32 = jnp.float32
BF16 = jnp.bfloat16
NT = (((1,), (1,)), ((), ()))
VMEM_LIMIT = 32 * 2**20

CROSS = 2.0 * BETA / WIDTH * LOG2E
ROW = -BETA / WIDTH * LOG2E
TOP = 2.0 * BETA * LOG2E


def split3(value):
    high = value.astype(BF16)
    rest = value - high.astype(F32)
    middle = rest.astype(BF16)
    low = (rest - middle.astype(F32)).astype(BF16)
    return high, middle, low


def own_turn():
    return (lax.axis_index("rep") + lax.axis_index("blk")) % 4


def pack_body(counts_ref, embeddings_ref, validity_ref, message_ref, live_ref, count_ref, sems):
    turn = own_turn()
    copies = [
        pltpu.make_async_copy(
            embeddings_ref.at[pl.ds(pl.multiple_of((4 * k + turn) * GRANULE, GRANULE), GRANULE), :],
            message_ref.at[pl.ds(k * GRANULE, GRANULE), :],
            sems.at[k],
        )
        for k in range(4)
    ]
    copies.append(pltpu.make_async_copy(counts_ref, count_ref, sems.at[4]))
    copies.append(pltpu.make_async_copy(validity_ref, live_ref, sems.at[5]))
    for copy in copies:
        copy.start()
    for copy in copies:
        copy.wait()
    rows = message_ref[:SHARE, :].astype(F32)
    square = rows * rows
    square = square[:, :GRANULE] + square[:, GRANULE:]
    norm = jnp.sum(square.T, axis=0, keepdims=True)
    shape = (SLOTS // GRANULE, GRANULE)
    position = lax.broadcasted_iota(jnp.int32, shape, 0) * GRANULE
    position = position + lax.broadcasted_iota(jnp.int32, shape, 1)
    live_ref[...] = jnp.where((position < count_ref[0]) & (live_ref[...] == 1), 1, 0)
    biases = []
    for k in range(4):
        live = live_ref[pl.ds(4 * k + turn, 1), :] == 1
        biases.append(jnp.where(live, TOP + ROW * norm[:, k * GRANULE : (k + 1) * GRANULE], DEAD))
    pairs = [jnp.concatenate(biases[:2], 1), jnp.concatenate(biases[2:], 1)]
    parts = [split3(pair) for pair in pairs]
    lines = [parts[h][level].astype(F32) for level in range(3) for h in range(2)]
    filled = jnp.clip((count_ref[0] // GRANULE - turn + 3) // 4, 0, 4)
    lines.append(jnp.full((EXTRA - 6, WIDTH), filled.astype(F32)))
    message_ref[SHARE:, :] = jnp.concatenate(lines, 0).astype(BF16)


def pack(counts, embeddings, validity):
    vmem = pl.BlockSpec(memory_space=pltpu.VMEM)
    return pl.pallas_call(
        pack_body,
        in_specs=[pl.BlockSpec(memory_space=pl.ANY)] * 3,
        out_specs=(vmem, vmem),
        out_shape=(
            jax.ShapeDtypeStruct((SHARE + EXTRA, WIDTH), BF16),
            jax.ShapeDtypeStruct((SLOTS // GRANULE, GRANULE), jnp.int32),
        ),
        scratch_shapes=[pltpu.SMEM((1,), jnp.int32), pltpu.SemaphoreType.DMA((6,))],
        compiler_params=pltpu.CompilerParams(vmem_limit_bytes=53 * 2**20),
        name="pack",
    )(counts, embeddings, validity.reshape(SLOTS // GRANULE, GRANULE))


def query_bias(query):
    wide = query.astype(F32)
    return jnp.sum(wide * wide, axis=1, keepdims=True) * ROW


def first_body(query_ref, message_ref, total_ref, weighted_ref, bias_ref):
    query = query_ref[...]
    row_bias = jnp.broadcast_to(query_bias(query), (TILE, GRANULE))
    bias_ref[...] = row_bias
    row_bias = jnp.concatenate([row_bias, row_bias], 1)
    extra = message_ref[SHARE:, :].astype(F32)
    half = SHARE // 2
    shape = (TILE, GRANULE)
    offset = lax.broadcasted_iota(jnp.int32, shape, 0) - lax.broadcasted_iota(jnp.int32, shape, 1)
    shift = own_turn() * GRANULE
    for h in range(2):
        rows = message_ref[h * half : (h + 1) * half, :]
        bias = extra[h : h + 1] + extra[2 + h : 3 + h] + extra[4 + h : 5 + h]
        gram = lax.dot_general(query, rows, NT, preferred_element_type=F32)
        kernel = jnp.exp2(gram * CROSS + (row_bias + bias))
        pieces = []
        for j in range(2):
            here = jnp.where(pl.program_id(0) == 2 * h + j, shift, SLOTS)
            piece = kernel[:, j * GRANULE : (j + 1) * GRANULE]
            pieces.append(jnp.where(offset == here, 0.0, piece))
        kernel = jnp.concatenate(pieces, 1)
        total = pieces[0] + pieces[1]
        weighted = jnp.dot(kernel.astype(BF16), rows, preferred_element_type=F32)
        if h == 0:
            total_ref[...] = total
            weighted_ref[...] = weighted
        else:
            total_ref[...] += total
            weighted_ref[...] += weighted


def cut(begin, size):
    step = TILE if size % TILE == 0 else size // 2
    return [slice(at, at + step) for at in range(begin, begin + size, step)]


def collect(messages, rows_ref, cols_ref):
    rows_ref[...] = jnp.zeros_like(rows_ref)
    cols_ref[...] = jnp.full_like(cols_ref, DEAD)
    place = jnp.int32(0)
    for message_ref in messages:
        extra = message_ref[SHARE:, :].astype(F32)
        filled = jnp.max(extra[6:7]).astype(jnp.int32)
        for k in range(4):
            start = pl.multiple_of((place + k) * GRANULE, GRANULE)
            rows_ref[pl.ds(start, GRANULE), :] = message_ref[k * GRANULE : (k + 1) * GRANULE, :]
            h, lanes = k // 2, slice((k % 2) * GRANULE, (k % 2 + 1) * GRANULE)
            bias = extra[h : h + 1, lanes] + extra[2 + h : 3 + h, lanes] + extra[4 + h : 5 + h, lanes]
            cols_ref[pl.ds(place + k, 1), :] = bias
        place = place + filled
    return (place + 1) // 2


def accumulate(pairs, chunks, base, query_ref, bias_ref, rows_ref, cols_ref, total_ref, weighted_ref):
    def run(begin, count):
        for i in range(count):
            pair = begin + i
            start = pl.multiple_of(pair * 2 * GRANULE, 2 * GRANULE)
            rows = rows_ref[pl.ds(start, 2 * GRANULE), :]
            bias = [cols_ref[pl.ds(2 * pair + j, 1), :] for j in range(2)]
            bias = jnp.concatenate(bias, 1)
            for here in chunks:
                there = slice(here.start - base, here.stop - base)
                row_bias = bias_ref[here, :]
                row_bias = jnp.concatenate([row_bias, row_bias], 1)
                gram = lax.dot_general(query_ref[here, :], rows, NT, preferred_element_type=F32)
                kernel = jnp.exp2(gram * CROSS + (row_bias + bias))
                total_ref[there, :] += kernel[:, :GRANULE] + kernel[:, GRANULE:]
                weighted_ref[there, :] += jnp.dot(
                    kernel.astype(BF16), rows, preferred_element_type=F32
                )

    done = jnp.int32(0)
    for count in (4, 2, 1):
        fits = pairs - done >= count
        pl.when(fits)(functools.partial(run, done, count))
        done = done + jnp.where(fits, count, 0)


def middle_body(shares, query_ref, bias_ref, total_in, weighted_in, *refs):
    messages, (total_ref, weighted_ref, rows_ref, cols_ref) = refs[:shares], refs[shares:]
    pairs = collect(messages, rows_ref, cols_ref)
    chunks = cut(0, SLOTS)
    accumulate(pairs, chunks, 0, query_ref, bias_ref, rows_ref, cols_ref, total_ref, weighted_ref)


def last_body(shares, begin, size, query_ref, bias_ref, total_in, weighted_in, *refs):
    messages = refs[:shares]
    keep_ref, send_ref, rows_ref, cols_ref, total_ref, weighted_ref = refs[shares:]
    whole = slice(begin, begin + size)
    total_ref[...] = total_in[whole, :]
    weighted_ref[...] = weighted_in[whole, :]
    pairs = collect(messages, rows_ref, cols_ref)
    chunks = cut(begin, size)
    accumulate(
        pairs, chunks, begin, query_ref, bias_ref, rows_ref, cols_ref, total_ref, weighted_ref
    )
    core = lax.axis_index("rep") % 2
    for here in chunks:
        there = slice(here.start - begin, here.stop - begin)
        total = jnp.sum(total_ref[there, :].T, axis=0, keepdims=True)
        total = jnp.broadcast_to(total, (8, total.shape[1]))
        turned = weighted_ref[there, :].T
        quarter = [turned[PART * i : PART * (i + 1)] for i in range(4)]
        for half in range(2):
            first, second = quarter[2 * half], quarter[2 * half + 1]
            keep_ref[PART * half : PART * (half + 1), there] = jnp.where(core == 0, first, second)
            send_ref[PART * half : PART * (half + 1), there] = jnp.where(core == 0, second, first)
        keep_ref[2 * PART :, there] = total
        send_ref[2 * PART :, there] = total


def cost(shares):
    return pl.CostEstimate(
        flops=int(shares * 4 * SLOTS * SHARE * WIDTH),
        bytes_accessed=4 * SLOTS * (WIDTH + GRANULE) * 2,
        transcendentals=int(shares * SLOTS * SHARE),
    )


WHOLE = pl.BlockSpec(memory_space=pltpu.VMEM)
QUERY = pl.BlockSpec((TILE, WIDTH), lambda i: (i, 0))
TOTAL = pl.BlockSpec((TILE, GRANULE), lambda i: (i, 0))
MESSAGE = pl.BlockSpec((SHARE + EXTRA, WIDTH), lambda i: (0, 0))
SUMS = (
    jax.ShapeDtypeStruct((SLOTS, GRANULE), F32),
    jax.ShapeDtypeStruct((SLOTS, WIDTH), F32),
)
PARAMS = pltpu.CompilerParams(vmem_limit_bytes=VMEM_LIMIT)
SMALL = pltpu.CompilerParams(vmem_limit_bytes=16 * 2**20)


def first(query, message):
    return pl.pallas_call(
        first_body,
        grid=(SLOTS // TILE,),
        in_specs=[QUERY, MESSAGE],
        out_specs=(TOTAL, QUERY, TOTAL),
        out_shape=SUMS + (jax.ShapeDtypeStruct((SLOTS, GRANULE), F32),),
        compiler_params=PARAMS,
        cost_estimate=cost(1),
        name="first",
    )(query, message)


def line_up(shares):
    return [((4 * shares * GRANULE, WIDTH), BF16), ((4 * shares, GRANULE), F32)]


def middle(query, bias, sums, messages):
    shares = len(messages)
    return pl.pallas_call(
        functools.partial(middle_body, shares),
        in_specs=[WHOLE] * (4 + shares),
        out_specs=(WHOLE, WHOLE),
        out_shape=SUMS,
        scratch_shapes=[pltpu.VMEM(*spec) for spec in line_up(shares)],
        input_output_aliases={2: 0, 3: 1},
        compiler_params=PARAMS,
        cost_estimate=cost(shares),
        name="middle",
    )(query, bias, *sums, *messages)


def last(query, bias, sums, messages, begin, size):
    shares = len(messages)
    shape = jax.ShapeDtypeStruct((2 * PART + 8, size), F32)
    scratch = line_up(shares) + [((size, GRANULE), F32), ((size, WIDTH), F32)]
    return pl.pallas_call(
        functools.partial(last_body, shares, begin, size),
        in_specs=[WHOLE] * (4 + shares),
        out_specs=(WHOLE, WHOLE),
        out_shape=(shape, shape),
        scratch_shapes=[pltpu.VMEM(*spec) for spec in scratch],
        compiler_params=PARAMS,
        cost_estimate=cost(len(messages) * size / SLOTS),
        name="last",
    )(query, bias, *sums, *messages)


def join_body(keep_ref, came_ref, *refs):
    *before, sum_ref, message_ref = refs
    size = keep_ref.shape[1]
    chip = lax.axis_index("rep") // 2
    both = keep_ref[...] + came_ref[...]
    low, high = both[:PART], both[PART : 2 * PART]
    total = both[2 * PART :]
    sum_ref[:PART, :] = jnp.where(chip == 0, low, high)
    sum_ref[PART:, :] = total
    message_ref[:, :size] = jnp.where(chip == 0, high, low).astype(BF16)
    if message_ref.shape[1] > size:
        totals = [ref[PART : PART + 1, :] for ref in before] + [total[:1]]
        totals = jnp.concatenate(totals, 1)
        lines = SLOTS // GRANULE
        totals = jnp.concatenate(
            [totals[:, i * GRANULE : (i + 1) * GRANULE] for i in range(lines)], 0
        )
        parts = [part.astype(F32) for part in split3(totals)]
        parts.append(jnp.zeros((PART - 3 * lines, GRANULE), F32))
        message_ref[:, size:] = jnp.concatenate(parts, 0).astype(BF16)


def join(keep, came, before, final):
    size = keep.shape[1]
    more = GRANULE if final else 0
    before = before if final else ()
    return pl.pallas_call(
        join_body,
        in_specs=[WHOLE] * (2 + len(before)),
        out_specs=[WHOLE] * 2,
        out_shape=(
            jax.ShapeDtypeStruct((PART + 8, size), F32),
            jax.ShapeDtypeStruct((PART, size + more), BF16),
        ),
        compiler_params=SMALL,
        cost_estimate=pl.CostEstimate(flops=10**6, bytes_accessed=3 * 10**6, transcendentals=0),
        name="join",
    )(keep, came, *before)


def finish_body(live_ref, *refs):
    halves, (log_ref, mean_ref) = refs[:-2], refs[-2:]
    lines = SLOTS // GRANULE
    extra = halves[-1][:, PIECES[-1] :].astype(F32)
    others = extra[:lines] + extra[lines : 2 * lines] + extra[2 * lines : 3 * lines]
    begin = 0
    for part, size in enumerate(PIECES):
        sum_ref, came_ref = halves[2 * part : 2 * part + 2]
        columns = slice(begin, begin + size)
        line = range(begin // GRANULE, (begin + size) // GRANULE)
        begin += size
        total = jnp.concatenate([others[i : i + 1] for i in line], 1)
        total = sum_ref[PART : PART + 1, :] + total
        live = live_ref[:, columns].astype(F32)
        shifted = total + EPSILON
        log_ref[:, columns] = live * jnp.log(shifted)
        scale = live / shifted
        mean_ref[:, columns] = (sum_ref[:PART, :] + came_ref[:, :size].astype(F32)) * scale


def finish(live, halves):
    vmem = pl.BlockSpec(memory_space=pltpu.VMEM)
    return pl.pallas_call(
        finish_body,
        in_specs=[vmem] * (1 + 2 * len(PIECES)),
        out_specs=(vmem, vmem),
        out_shape=(
            jax.ShapeDtypeStruct((1, SLOTS), F32),
            jax.ShapeDtypeStruct((PART, SLOTS), F32),
        ),
        compiler_params=SMALL,
        name="finish",
    )(live.reshape(1, SLOTS), *halves)


def route(blocks, reps, move):
    pairs = []
    for block in range(blocks):
        for rep in range(reps):
            row, column = divmod(block, 2)
            (row_to, column_to), rep_to = move(row, column, rep)
            block_to = (row_to * 2 + column_to) % blocks
            pairs.append((block * reps + rep, block_to * reps + rep_to))
    return pairs


def on_device(embeddings, counts, validity):
    blocks, reps = lax.axis_size("blk"), lax.axis_size("rep")

    def send(value, move):
        return lax.ppermute(value, ("blk", "rep"), route(blocks, reps, move))

    ahead = lambda m, h, r: ((m + 2 * h - 1, h), r)
    behind = lambda m, h, r: ((m + 1 - 2 * h, h), r)
    across = lambda m, h, r: ((m, 1 - h), r ^ 2)
    corner = lambda m, h, r: ((m + 2 * h - 1, 1 - h), r ^ 2)
    other_core = lambda m, h, r: ((m, h), r ^ 1)
    other_chip = lambda m, h, r: ((m, h), r ^ 2)

    mine, live = pack(counts, embeddings, validity)
    from_across = send(mine, across)
    from_ahead = send(mine, ahead)
    from_behind = send(mine, behind)
    *sums, bias = first(embeddings, mine)
    far = send(from_ahead, corner)
    side = send(from_ahead, across)
    near = send(from_across, ahead)
    sums = middle(embeddings, bias, sums, (from_across, from_ahead, from_behind))
    sums = middle(embeddings, bias, sums, (far,))
    halves, begin = [], 0
    for size in PIECES:
        keep, give = last(embeddings, bias, sums, (side, near), begin, size)
        begin += size
        summed, message = join(keep, send(give, other_core), halves[::2], begin == SLOTS)
        halves += [summed, send(message, other_chip)]
    log_density, mean = finish(live, halves)
    return log_density.reshape(SLOTS), mean.T


def solution(mesh):
    return jax.shard_map(
        on_device,
        mesh=mesh,
        in_specs=(P("blk", None), P("blk"), P("blk")),
        out_specs=(P("blk"), P("blk", "rep")),
        check_vma=False,
    )
```

profile of v0, /device:TPU:4, one launch (start us, length us, event | category | flops | bytes accessed | tf_op | source)
XLA Modules:
  0.0 48.7 jit_solution(7238953094910762220)
XLA Ops:
  1.3 0.0 copy-start.1
  1.3 0.7 %copy-done.1 = s32[2048]{0:T(1024)S(1)} copy-done((s32[2048]{0:T(1024)S(1)}, s32[2048]{0:T(1024)}, u32[]{:S(2)}) %copy-start.1) | copy-done | bytes 8216
  2.0 1.2 %pack.1 = (bf16[520,256]{1,0:T(8,128)(2,1)S(1)}, s32[16,128]{1,0:T(8,128)S(1)}) custom-call(s32[1]{0:T(128)S(6)} %copy.13.counts_ref, bf16[2048,256]{1,0:T(8,128)(2,1)} %query_ref.9, s32[16,128]{1,0:T(8,128)S(1)} %bitcast.4), custom_call_target="tpu_custom_call" | custom-call | tf_op jit(solution)/shard_map/pack/pallas_call | solution.py:85
  3.1 2.0 %collective-permute-start.1 = (bf16[520,256]{1,0:T(8,128)(2,1)S(1)}, bf16[520,256]{1,0:T(8,128)(2,1)S(1)}, u32[]{:S(2)}, u32[]{:S(2)}) collective-permute-start(bf16[520,256]{1,0:T(8,128)(2,1)S(1)} %get-tuple-element.22.message_ref), channel_id=1, source_target_pairs={{0,248},{1,249},{2,250},{3,251},{4,12},{5,13},{6,14},{7,15},{8,0},... | collective-permute-start | bytes 798728 | tf_op jit(solution)/shard_map/ppermute | solution.py:374
  5.1 6.9 %collective-permute-start = (bf16[520,256]{1,0:T(8,128)(2,1)S(1)}, bf16[520,256]{1,0:T(8,128)(2,1)S(1)}, u32[]{:S(2)}, u32[]{:S(2)}) collective-permute-start(bf16[520,256]{1,0:T(8,128)(2,1)S(1)} %get-tuple-element.22.message_ref), channel_id=1, source_target_pairs={{0,6},{1,7},{2,4},{3,5},{4,2},{5,3},{6,0},{7,1},{8,14},{9,15},{10,... | collective-permute-start | bytes 798728 | tf_op jit(solution)/shard_map/ppermute | solution.py:374
  12.1 1.0 %collective-permute-start.2 = (bf16[520,256]{1,0:T(8,128)(2,1)S(1)}, bf16[520,256]{1,0:T(8,128)(2,1)S(1)}, u32[]{:S(2)}, u32[]{:S(2)}) collective-permute-start(bf16[520,256]{1,0:T(8,128)(2,1)S(1)} %get-tuple-element.22.message_ref), channel_id=1, source_target_pairs={{0,8},{1,9},{2,10},{3,11},{4,252},{5,253},{6,254},{7,255},{8,16},{... | collective-permute-start | bytes 798728 | tf_op jit(solution)/shard_map/ppermute | solution.py:374
  13.1 0.0 copy-start
  13.1 1.2 %copy-done = bf16[2048,256]{1,0:T(8,128)(2,1)S(1)} copy-done((bf16[2048,256]{1,0:T(8,128)(2,1)S(1)}, bf16[2048,256]{1,0:T(8,128)(2,1)}, u32[]{:S(2)}) %copy-start) | copy-done | bytes 1048600
  14.3 2.9 %first.1 = (f32[2048,128]{1,0:T(8,128)S(1)}, f32[2048,256]{1,0:T(8,128)S(1)}, f32[2048,128]{1,0:T(8,128)S(1)}) custom-call(bf16[2048,256]{1,0:T(8,128)(2,1)S(1)} %copy-done, bf16[520,256]{1,0:T(8,128)(2,1)S(1)} %get-tuple-element.22.message_ref), custom_call_target="tpu_custom_call" | custom-call | flops 1073741824 | bytes 6291456 | tf_op jit(solution)/shard_map/first/pallas_call | solution.py:237
  17.2 0.8 %collective-permute-done.1.refs_1_ = bf16[520,256]{1,0:T(8,128)(2,1)S(1)} collective-permute-done((bf16[520,256]{1,0:T(8,128)(2,1)S(1)}, bf16[520,256]{1,0:T(8,128)(2,1)S(1)}, u32[]{:S(2)}, u32[]{:S(2)}) %collective-permute-start.1) | collective-permute-done | bytes 266272 | tf_op jit(solution)/shard_map/ppermute | solution.py:374
  17.9 0.0 collective-permute-start.3
  17.9 3.2 %collective-permute-start.4 = (bf16[520,256]{1,0:T(8,128)(2,1)S(1)}, bf16[520,256]{1,0:T(8,128)(2,1)S(1)}, u32[]{:S(2)}, u32[]{:S(2)}) collective-permute-start(bf16[520,256]{1,0:T(8,128)(2,1)S(1)} %collective-permute-done.1.refs_1_), channel_id=1, source_target_pairs={{0,6},{1,7},{2,4},{3,5},{4,2},{5,3},{6,0},{7,1},{8,14},{9,15},{10,... | collective-permute-start | bytes 798728 | tf_op jit(solution)/shard_map/ppermute | solution.py:374
  21.1 0.0 collective-permute-done.refs_0_
  21.1 0.3 collective-permute-start.5
  21.4 0.0 collective-permute-done.2.refs_2_
  21.4 2.9 %middle.2 = (f32[2048,128]{1,0:T(8,128)S(1)}, f32[2048,256]{1,0:T(8,128)S(1)}) custom-call(bf16[2048,256]{1,0:T(8,128)(2,1)S(1)} %copy-done, f32[2048,128]{1,0:T(8,128)S(1)} %get-tuple-element.23.bias_ref, f32[2048,128]{1,0:T(8,128)S(1)} %get-tuple-element.24.total_in, ...), custom_call_target="tpu_custom_call", output_to_operand_aliasing={{0}: (2, {}), {1}: (3, {})} | custom-call | flops 3221225472 | bytes 6291456 | tf_op jit(solution)/shard_map/middle/pallas_call | solution.py:255
  24.3 3.9 %collective-permute-done.3.refs_0_ = bf16[520,256]{1,0:T(8,128)(2,1)S(1)} collective-permute-done((bf16[520,256]{1,0:T(8,128)(2,1)S(1)}, bf16[520,256]{1,0:T(8,128)(2,1)S(1)}, u32[]{:S(2)}, u32[]{:S(2)}) %collective-permute-start.3) | collective-permute-done | bytes 266272 | tf_op jit(solution)/shard_map/ppermute | solution.py:374
  28.1 2.0 %middle.3 = (f32[2048,128]{1,0:T(8,128)S(1)}, f32[2048,256]{1,0:T(8,128)S(1)}) custom-call(bf16[2048,256]{1,0:T(8,128)(2,1)S(1)} %copy-done, f32[2048,128]{1,0:T(8,128)S(1)} %get-tuple-element.23.bias_ref, f32[2048,128]{1,0:T(8,128)S(1)} %get-tuple-element.26.total_in, ...), custom_call_target="tpu_custom_call", output_to_operand_aliasing={{0}: (2, {}), {1}: (3, {})} | custom-call | flops 1073741824 | bytes 6291456 | tf_op jit(solution)/shard_map/middle/pallas_call | solution.py:255
  30.1 1.9 %collective-permute-done.4.refs_0_ = bf16[520,256]{1,0:T(8,128)(2,1)S(1)} collective-permute-done((bf16[520,256]{1,0:T(8,128)(2,1)S(1)}, bf16[520,256]{1,0:T(8,128)(2,1)S(1)}, u32[]{:S(2)}, u32[]{:S(2)}) %collective-permute-start.4) | collective-permute-done | bytes 266272 | tf_op jit(solution)/shard_map/ppermute | solution.py:374
  32.1 1.4 %collective-permute-done.5.refs_1_ = bf16[520,256]{1,0:T(8,128)(2,1)S(1)} collective-permute-done((bf16[520,256]{1,0:T(8,128)(2,1)S(1)}, bf16[520,256]{1,0:T(8,128)(2,1)S(1)}, u32[]{:S(2)}, u32[]{:S(2)}) %collective-permute-start.5) | collective-permute-done | bytes 266272 | tf_op jit(solution)/shard_map/ppermute | solution.py:374
  33.5 2.7 %last.2 = (f32[136,1280]{1,0:T(8,128)S(1)}, f32[136,1280]{1,0:T(8,128)S(1)}) custom-call(bf16[2048,256]{1,0:T(8,128)(2,1)S(1)} %copy-done, f32[2048,128]{1,0:T(8,128)S(1)} %get-tuple-element.23.bias_ref, f32[2048,128]{1,0:T(8,128)S(1)} %get-tuple-element.28.total_in, f32[2048,256]{1,0:T(8,128)S(1)} %get-tuple-element.29.weighted_in, ...), custom_call_target="tpu_custom_call" | custom-call | flops 1342177280 | bytes 6291456 | tf_op jit(solution)/shard_map/last/pallas_call | solution.py:272
  36.2 0.1 collective-permute-start.6
  36.3 2.1 %last.3 = (f32[136,768]{1,0:T(8,128)S(1)}, f32[136,768]{1,0:T(8,128)S(1)}) custom-call(bf16[2048,256]{1,0:T(8,128)(2,1)S(1)} %copy-done, f32[2048,128]{1,0:T(8,128)S(1)} %get-tuple-element.23.bias_ref, f32[2048,128]{1,0:T(8,128)S(1)} %get-tuple-element.28.total_in, f32[2048,256]{1,0:T(8,128)S(1)} %get-tuple-element.29.weighted_in, ...), custom_call_target="tpu_custom_call" | custom-call | flops 805306368 | bytes 6291456 | tf_op jit(solution)/shard_map/last/pallas_call | solution.py:272
  38.4 0.1 collective-permute-start.8
  38.5 0.0 collective-permute-done.6.came_ref
  38.5 0.1 join.2
  38.6 0.4 collective-permute-start.7
  39.0 1.3 %collective-permute-done.8.came_ref = f32[136,768]{1,0:T(8,128)S(1)} collective-permute-done((f32[136,768]{1,0:T(8,128)S(1)}, f32[136,768]{1,0:T(8,128)S(1)}, u32[]{:S(2)}, u32[]{:S(2)}) %collective-permute-start.8) | collective-permute-done | bytes 417824 | tf_op jit(solution)/shard_map/ppermute | solution.py:374
  40.3 0.1 join.3
  40.3 0.6 %collective-permute-start.9 = (bf16[64,896]{1,0:T(8,128)(2,1)S(1)}, bf16[64,896]{1,0:T(8,128)(2,1)S(1)}, u32[]{:S(2)}, u32[]{:S(2)}) collective-permute-start(bf16[64,896]{1,0:T(8,128)(2,1)S(1)} %get-tuple-element.37), channel_id=1, source_target_pairs={{0,2},{1,3},{2,0},{3,1},{4,6},{5,7},{6,4},{7,5},{8,10},{9,11},{10,... | collective-permute-start | bytes 344072 | tf_op jit(solution)/shard_map/ppermute | solution.py:374
  40.9 6.9 %collective-permute-done.9.refs_3_ = bf16[64,896]{1,0:T(8,128)(2,1)S(1)} collective-permute-done((bf16[64,896]{1,0:T(8,128)(2,1)S(1)}, bf16[64,896]{1,0:T(8,128)(2,1)S(1)}, u32[]{:S(2)}, u32[]{:S(2)}) %collective-permute-start.9) | collective-permute-done | bytes 114720 | tf_op jit(solution)/shard_map/ppermute | solution.py:374
  47.8 0.0 collective-permute-done.7.refs_1_
  47.8 0.9 %finish.1 = (f32[1,2048]{1,0:T(1,128)}, f32[64,2048]{1,0:T(8,128)}) custom-call(s32[1,2048]{1,0:T(1,128)S(1)} %bitcast.5, f32[72,1280]{1,0:T(8,128)S(1)} %get-tuple-element.32.refs_0_, bf16[64,1280]{1,0:T(8,128)(2,1)S(1)} %collective-permute-done.7.refs_1_, f32[72,768]{1,0:T(8,128)S(1)} %get-tuple-element.36.refs_2_, ...), custom_call_target="tpu_custom_call" | custom-call | tf_op jit(solution)/shard_map/finish/pallas_call | solution.py:346
Async XLA Ops:
  1.3 0.7 %copy-start.1 = (s32[2048]{0:T(1024)S(1)}, s32[2048]{0:T(1024)}, u32[]{:S(2)}) copy-start(s32[2048]{0:T(1024)} %param.5) | copy-start | bytes 24580
  3.1 14.8 %collective-permute-start.1 = (bf16[520,256]{1,0:T(8,128)(2,1)S(1)}, bf16[520,256]{1,0:T(8,128)(2,1)S(1)}, u32[]{:S(2)}, u32[]{:S(2)}) collective-permute-start(bf16[520,256]{1,0:T(8,128)(2,1)S(1)} %get-tuple-element.22.message_ref), channel_id=1, source_target_pairs={{0,248},{1,249},{2,250},{3,251},{4,12},{5,13},{6,14},{7,15},{8,0},... | collective-permute-start | bytes 798728 | tf_op jit(solution)/shard_map/ppermute | solution.py:374
  5.1 16.0 %collective-permute-start = (bf16[520,256]{1,0:T(8,128)(2,1)S(1)}, bf16[520,256]{1,0:T(8,128)(2,1)S(1)}, u32[]{:S(2)}, u32[]{:S(2)}) collective-permute-start(bf16[520,256]{1,0:T(8,128)(2,1)S(1)} %get-tuple-element.22.message_ref), channel_id=1, source_target_pairs={{0,6},{1,7},{2,4},{3,5},{4,2},{5,3},{6,0},{7,1},{8,14},{9,15},{10,... | collective-permute-start | bytes 798728 | tf_op jit(solution)/shard_map/ppermute | solution.py:374
  12.1 9.4 %collective-permute-start.2 = (bf16[520,256]{1,0:T(8,128)(2,1)S(1)}, bf16[520,256]{1,0:T(8,128)(2,1)S(1)}, u32[]{:S(2)}, u32[]{:S(2)}) collective-permute-start(bf16[520,256]{1,0:T(8,128)(2,1)S(1)} %get-tuple-element.22.message_ref), channel_id=1, source_target_pairs={{0,8},{1,9},{2,10},{3,11},{4,252},{5,253},{6,254},{7,255},{8,16},{... | collective-permute-start | bytes 798728 | tf_op jit(solution)/shard_map/ppermute | solution.py:374
  13.1 1.2 %copy-start = (bf16[2048,256]{1,0:T(8,128)(2,1)S(1)}, bf16[2048,256]{1,0:T(8,128)(2,1)}, u32[]{:S(2)}) copy-start(bf16[2048,256]{1,0:T(8,128)(2,1)} %query_ref.9) | copy-start | bytes 3145732
  17.9 10.2 %collective-permute-start.3 = (bf16[520,256]{1,0:T(8,128)(2,1)S(1)}, bf16[520,256]{1,0:T(8,128)(2,1)S(1)}, u32[]{:S(2)}, u32[]{:S(2)}) collective-permute-start(bf16[520,256]{1,0:T(8,128)(2,1)S(1)} %collective-permute-done.1.refs_1_), channel_id=1, source_target_pairs={{0,254},{1,255},{2,252},{3,253},{4,10},{5,11},{6,8},{7,9},{8,6},{9... | collective-permute-start | bytes 798728 | tf_op jit(solution)/shard_map/ppermute | solution.py:374
  17.9 14.1 %collective-permute-start.4 = (bf16[520,256]{1,0:T(8,128)(2,1)S(1)}, bf16[520,256]{1,0:T(8,128)(2,1)S(1)}, u32[]{:S(2)}, u32[]{:S(2)}) collective-permute-start(bf16[520,256]{1,0:T(8,128)(2,1)S(1)} %collective-permute-done.1.refs_1_), channel_id=1, source_target_pairs={{0,6},{1,7},{2,4},{3,5},{4,2},{5,3},{6,0},{7,1},{8,14},{9,15},{10,... | collective-permute-start | bytes 798728 | tf_op jit(solution)/shard_map/ppermute | solution.py:374
  21.1 12.4 %collective-permute-start.5 = (bf16[520,256]{1,0:T(8,128)(2,1)S(1)}, bf16[520,256]{1,0:T(8,128)(2,1)S(1)}, u32[]{:S(2)}, u32[]{:S(2)}) collective-permute-start(bf16[520,256]{1,0:T(8,128)(2,1)S(1)} %collective-permute-done.refs_0_), channel_id=1, source_target_pairs={{0,248},{1,249},{2,250},{3,251},{4,12},{5,13},{6,14},{7,15},{8,0},... | collective-permute-start | bytes 798728 | tf_op jit(solution)/shard_map/ppermute | solution.py:374
  36.2 2.3 %collective-permute-start.6 = (f32[136,1280]{1,0:T(8,128)S(1)}, f32[136,1280]{1,0:T(8,128)S(1)}, u32[]{:S(2)}, u32[]{:S(2)}) collective-permute-start(f32[136,1280]{1,0:T(8,128)S(1)} %get-tuple-element.31), channel_id=1, source_target_pairs={{0,1},{1,0},{2,3},{3,2},{4,5},{5,4},{6,7},{7,6},{8,9},{9,8},{10,11... | collective-permute-start | bytes 2088968 | tf_op jit(solution)/shard_map/ppermute | solution.py:374
  38.4 1.8 %collective-permute-start.8 = (f32[136,768]{1,0:T(8,128)S(1)}, f32[136,768]{1,0:T(8,128)S(1)}, u32[]{:S(2)}, u32[]{:S(2)}) collective-permute-start(f32[136,768]{1,0:T(8,128)S(1)} %get-tuple-element.35), channel_id=1, source_target_pairs={{0,1},{1,0},{2,3},{3,2},{4,5},{5,4},{6,7},{7,6},{8,9},{9,8},{10,11... | collective-permute-start | bytes 1253384 | tf_op jit(solution)/shard_map/ppermute | solution.py:374
  38.6 9.1 %collective-permute-start.7 = (bf16[64,1280]{1,0:T(8,128)(2,1)S(1)}, bf16[64,1280]{1,0:T(8,128)(2,1)S(1)}, u32[]{:S(2)}, u32[]{:S(2)}) collective-permute-start(bf16[64,1280]{1,0:T(8,128)(2,1)S(1)} %get-tuple-element.33), channel_id=1, source_target_pairs={{0,2},{1,3},{2,0},{3,1},{4,6},{5,7},{6,4},{7,5},{8,10},{9,11},{10,... | collective-permute-start | bytes 491528 | tf_op jit(solution)/shard_map/ppermute | solution.py:374
  40.3 7.4 %collective-permute-start.9 = (bf16[64,896]{1,0:T(8,128)(2,1)S(1)}, bf16[64,896]{1,0:T(8,128)(2,1)S(1)}, u32[]{:S(2)}, u32[]{:S(2)}) collective-permute-start(bf16[64,896]{1,0:T(8,128)(2,1)S(1)} %get-tuple-element.37), channel_id=1, source_target_pairs={{0,2},{1,3},{2,0},{3,1},{4,6},{5,7},{6,4},{7,5},{8,10},{9,11},{10,... | collective-permute-start | bytes 344072 | tf_op jit(solution)/shard_map/ppermute | solution.py:374
where the time goes:
time: 48.9 us; the launch traced here: 48.7 us
  waiting for transfers between devices  16.1 us (33%)
  Pallas kernels  14.7 us (30%)
  starting transfers between devices  14.5 us (30%)
  local copies, waits for them, and re-layouts  1.91 us (4%)
  between operations  1.37 us (3%)
    ppermute x10, waiting for transfers between devices, send(): return lax.ppermute(value, ('blk', 'rep'), route(blocks, reps, move))  16.1 us
    ppermute x10, starting transfers between devices, send(): return lax.ppermute(value, ('blk', 'rep'), route(blocks, reps, move))  14.5 us
    pallas_call x2, Pallas kernels, middle(): pl.pallas_call(functools.partial(middle_body, shares), in_specs=[WHOLE] *...  4.83 us
    pallas_call x2, Pallas kernels, last(): pl.pallas_call(functools.partial(last_body, shares, begin, size), in_spec...  4.82 us
    pallas_call x1, Pallas kernels, first(): pl.pallas_call(first_body, grid=(SLOTS // TILE,), in_specs=[QUERY, MESSAG...  2.86 us
    unnamed x4, local copies, waits for them, and re-layouts  1.91 us
    pallas_call x1, Pallas kernels, pack(): pl.pallas_call(pack_body, in_specs=[pl.BlockSpec(memory_space=pl.ANY)] *...  1.15 us
  transfers between devices with their start and end apart: 10, of which 6 were waited for; matrix products, arithmetic and copies ran while one was open for 0% of the time, Pallas kernels for 20%

commit v1 on v0

--- a/solution.py
+++ b/solution.py
@@ -17,7 +17,7 @@
 WIDTH = 256
 SHARE = 512
 GRANULE = 128
-EXTRA = 8
+EXTRA = 16
 TILE = 512
 PART = 64
 PIECES = (1280, 768)
@@ -174,7 +174,8 @@
                 )
 
     done = jnp.int32(0)
-    for count in (4, 2, 1):
+    room = rows_ref.shape[0] // (2 * GRANULE)
+    for count in [count for count in (4, 2, 1) if count <= room]:
         fits = pairs - done >= count
         pl.when(fits)(functools.partial(run, done, count))
         done = done + jnp.where(fits, count, 0)

time: 48.9 us -> 49.8 us (1.018)
  the two profiles are of different devices: /device:TPU:4 before, /device:TPU:1 now
where the time goes in v1:
time: 49.8 us; the launch traced here: 49.6 us
  starting transfers between devices  19.8 us (40%)
  Pallas kernels  13.2 us (27%)
  waiting for transfers between devices  13.2 us (27%)
  local copies, waits for them, and re-layouts  1.91 us (4%)
  between operations  1.36 us (3%)
    ppermute x10, starting transfers between devices, send(): return lax.ppermute(value, ('blk', 'rep'), route(blocks, reps, move))  19.8 us
    ppermute x10, waiting for transfers between devices, send(): return lax.ppermute(value, ('blk', 'rep'), route(blocks, reps, move))  13.2 us
    pallas_call x2, Pallas kernels, middle(): pl.pallas_call(functools.partial(middle_body, shares), in_specs=[WHOLE] *...  4.78 us
    pallas_call x2, Pallas kernels, last(): pl.pallas_call(functools.partial(last_body, shares, begin, size), in_spec...  3.38 us
    pallas_call x1, Pallas kernels, first(): pl.pallas_call(first_body, grid=(SLOTS // TILE,), in_specs=[QUERY, MESSAG...  2.88 us
    unnamed x4, local copies, waits for them, and re-layouts  1.91 us
    pallas_call x1, Pallas kernels, pack(): pl.pallas_call(pack_body, in_specs=[pl.BlockSpec(memory_space=pl.ANY)] *...  1.15 us
  transfers between devices with their start and end apart: 10, of which 5 were waited for; matrix products, arithmetic and copies ran while one was open for 0% of the time, Pallas kernels for 19%

profile of v1, /device:TPU:1, one launch (start us, length us, event | category | flops | bytes accessed | tf_op | source)
XLA Modules:
  0.0 49.6 jit_solution(16167424702506919683)
XLA Ops:
  1.3 0.0 copy-start.1
  1.3 0.7 %copy-done.1 = s32[2048]{0:T(1024)S(1)} copy-done((s32[2048]{0:T(1024)S(1)}, s32[2048]{0:T(1024)}, u32[]{:S(2)}) %copy-start.1) | copy-done | bytes 8216
  2.0 1.2 %pack.1 = (bf16[528,256]{1,0:T(8,128)(2,1)S(1)}, s32[16,128]{1,0:T(8,128)S(1)}) custom-call(s32[1]{0:T(128)S(6)} %copy.13.counts_ref, bf16[2048,256]{1,0:T(8,128)(2,1)} %query_ref.9, s32[16,128]{1,0:T(8,128)S(1)} %bitcast.4), custom_call_target="tpu_custom_call" | custom-call | tf_op jit(solution)/shard_map/pack/pallas_call | solution.py:85
  3.1 8.9 %collective-permute-start.1 = (bf16[528,256]{1,0:T(8,128)(2,1)S(1)}, bf16[528,256]{1,0:T(8,128)(2,1)S(1)}, u32[]{:S(2)}, u32[]{:S(2)}) collective-permute-start(bf16[528,256]{1,0:T(8,128)(2,1)S(1)} %get-tuple-element.22.message_ref), channel_id=1, source_target_pairs={{0,248},{1,249},{2,250},{3,251},{4,12},{5,13},{6,14},{7,15},{8,0},... | collective-permute-start | bytes 811016 | tf_op jit(solution)/shard_map/ppermute | solution.py:375
  12.1 0.0 collective-permute-start
  12.1 0.0 collective-permute-start.2
  12.1 0.0 copy-start
  12.1 1.2 %copy-done = bf16[2048,256]{1,0:T(8,128)(2,1)S(1)} copy-done((bf16[2048,256]{1,0:T(8,128)(2,1)S(1)}, bf16[2048,256]{1,0:T(8,128)(2,1)}, u32[]{:S(2)}) %copy-start) | copy-done | bytes 1048600
  13.3 2.9 %first.1 = (f32[2048,128]{1,0:T(8,128)S(1)}, f32[2048,256]{1,0:T(8,128)S(1)}, f32[2048,128]{1,0:T(8,128)S(1)}) custom-call(bf16[2048,256]{1,0:T(8,128)(2,1)S(1)} %copy-done, bf16[528,256]{1,0:T(8,128)(2,1)S(1)} %get-tuple-element.22.message_ref), custom_call_target="tpu_custom_call" | custom-call | flops 1073741824 | bytes 6291456 | tf_op jit(solution)/shard_map/first/pallas_call | solution.py:238
  16.2 1.0 %collective-permute-done.1.refs_1_ = bf16[528,256]{1,0:T(8,128)(2,1)S(1)} collective-permute-done((bf16[528,256]{1,0:T(8,128)(2,1)S(1)}, bf16[528,256]{1,0:T(8,128)(2,1)S(1)}, u32[]{:S(2)}, u32[]{:S(2)}) %collective-permute-start.1) | collective-permute-done | bytes 270368 | tf_op jit(solution)/shard_map/ppermute | solution.py:375
  17.2 4.4 %collective-permute-start.3 = (bf16[528,256]{1,0:T(8,128)(2,1)S(1)}, bf16[528,256]{1,0:T(8,128)(2,1)S(1)}, u32[]{:S(2)}, u32[]{:S(2)}) collective-permute-start(bf16[528,256]{1,0:T(8,128)(2,1)S(1)} %collective-permute-done.1.refs_1_), channel_id=1, source_target_pairs={{0,254},{1,255},{2,252},{3,253},{4,10},{5,11},{6,8},{7,9},{8,6},{9... | collective-permute-start | bytes 811016 | tf_op jit(solution)/shard_map/ppermute | solution.py:375
  21.6 0.0 collective-permute-start.4
  21.6 0.0 collective-permute-done.refs_0_
  21.6 2.8 %collective-permute-start.5 = (bf16[528,256]{1,0:T(8,128)(2,1)S(1)}, bf16[528,256]{1,0:T(8,128)(2,1)S(1)}, u32[]{:S(2)}, u32[]{:S(2)}) collective-permute-start(bf16[528,256]{1,0:T(8,128)(2,1)S(1)} %collective-permute-done.refs_0_), channel_id=1, source_target_pairs={{0,248},{1,249},{2,250},{3,251},{4,12},{5,13},{6,14},{7,15},{8,0},... | collective-permute-start | bytes 811016 | tf_op jit(solution)/shard_map/ppermute | solution.py:375
  24.4 0.0 collective-permute-done.2.refs_2_
  24.4 2.8 %middle.2 = (f32[2048,128]{1,0:T(8,128)S(1)}, f32[2048,256]{1,0:T(8,128)S(1)}) custom-call(bf16[2048,256]{1,0:T(8,128)(2,1)S(1)} %copy-done, f32[2048,128]{1,0:T(8,128)S(1)} %get-tuple-element.23.bias_ref, f32[2048,128]{1,0:T(8,128)S(1)} %get-tuple-element.24.total_in, ...), custom_call_target="tpu_custom_call", output_to_operand_aliasing={{0}: (2, {}), {1}: (3, {})} | custom-call | flops 3221225472 | bytes 6291456 | tf_op jit(solution)/shard_map/middle/pallas_call | solution.py:256
  27.2 1.9 %collective-permute-done.3.refs_0_ = bf16[528,256]{1,0:T(8,128)(2,1)S(1)} collective-permute-done((bf16[528,256]{1,0:T(8,128)(2,1)S(1)}, bf16[528,256]{1,0:T(8,128)(2,1)S(1)}, u32[]{:S(2)}, u32[]{:S(2)}) %collective-permute-start.3) | collective-permute-done | bytes 270368 | tf_op jit(solution)/shard_map/ppermute | solution.py:375
  29.1 1.9 %middle.3 = (f32[2048,128]{1,0:T(8,128)S(1)}, f32[2048,256]{1,0:T(8,128)S(1)}) custom-call(bf16[2048,256]{1,0:T(8,128)(2,1)S(1)} %copy-done, f32[2048,128]{1,0:T(8,128)S(1)} %get-tuple-element.23.bias_ref, f32[2048,128]{1,0:T(8,128)S(1)} %get-tuple-element.26.total_in, ...), custom_call_target="tpu_custom_call", output_to_operand_aliasing={{0}: (2, {}), {1}: (3, {})} | custom-call | flops 1073741824 | bytes 6291456 | tf_op jit(solution)/shard_map/middle/pallas_call | solution.py:256
  31.1 2.5 %collective-permute-done.4.refs_0_ = bf16[528,256]{1,0:T(8,128)(2,1)S(1)} collective-permute-done((bf16[528,256]{1,0:T(8,128)(2,1)S(1)}, bf16[528,256]{1,0:T(8,128)(2,1)S(1)}, u32[]{:S(2)}, u32[]{:S(2)}) %collective-permute-start.4) | collective-permute-done | bytes 270368 | tf_op jit(solution)/shard_map/ppermute | solution.py:375
  33.6 0.0 collective-permute-done.5.refs_1_
  33.6 1.9 %last.2 = (f32[136,1280]{1,0:T(8,128)S(1)}, f32[136,1280]{1,0:T(8,128)S(1)}) custom-call(bf16[2048,256]{1,0:T(8,128)(2,1)S(1)} %copy-done, f32[2048,128]{1,0:T(8,128)S(1)} %get-tuple-element.23.bias_ref, f32[2048,128]{1,0:T(8,128)S(1)} %get-tuple-element.28.total_in, f32[2048,256]{1,0:T(8,128)S(1)} %get-tuple-element.29.weighted_in, ...), custom_call_target="tpu_custom_call" | custom-call | flops 1342177280 | bytes 6291456 | tf_op jit(solution)/shard_map/last/pallas_call | solution.py:273
  35.5 2.5 %collective-permute-start.6 = (f32[136,1280]{1,0:T(8,128)S(1)}, f32[136,1280]{1,0:T(8,128)S(1)}, u32[]{:S(2)}, u32[]{:S(2)}) collective-permute-start(f32[136,1280]{1,0:T(8,128)S(1)} %get-tuple-element.31), channel_id=1, source_target_pairs={{0,1},{1,0},{2,3},{3,2},{4,5},{5,4},{6,7},{7,6},{8,9},{9,8},{10,11... | collective-permute-start | bytes 2088968 | tf_op jit(solution)/shard_map/ppermute | solution.py:375
  38.0 1.4 %last.3 = (f32[136,768]{1,0:T(8,128)S(1)}, f32[136,768]{1,0:T(8,128)S(1)}) custom-call(bf16[2048,256]{1,0:T(8,128)(2,1)S(1)} %copy-done, f32[2048,128]{1,0:T(8,128)S(1)} %get-tuple-element.23.bias_ref, f32[2048,128]{1,0:T(8,128)S(1)} %get-tuple-element.28.total_in, f32[2048,256]{1,0:T(8,128)S(1)} %get-tuple-element.29.weighted_in, ...), custom_call_target="tpu_custom_call" | custom-call | flops 805306368 | bytes 6291456 | tf_op jit(solution)/shard_map/last/pallas_call | solution.py:273
  39.5 0.7 %collective-permute-start.8 = (f32[136,768]{1,0:T(8,128)S(1)}, f32[136,768]{1,0:T(8,128)S(1)}, u32[]{:S(2)}, u32[]{:S(2)}) collective-permute-start(f32[136,768]{1,0:T(8,128)S(1)} %get-tuple-element.35), channel_id=1, source_target_pairs={{0,1},{1,0},{2,3},{3,2},{4,5},{5,4},{6,7},{7,6},{8,9},{9,8},{10,11... | collective-permute-start | bytes 1253384 | tf_op jit(solution)/shard_map/ppermute | solution.py:375
  40.2 0.0 collective-permute-done.6.came_ref
  40.2 0.1 join.2
  40.3 0.1 collective-permute-start.7
  40.4 1.2 %collective-permute-done.8.came_ref = f32[136,768]{1,0:T(8,128)S(1)} collective-permute-done((f32[136,768]{1,0:T(8,128)S(1)}, f32[136,768]{1,0:T(8,128)S(1)}, u32[]{:S(2)}, u32[]{:S(2)}) %collective-permute-start.8) | collective-permute-done | bytes 417824 | tf_op jit(solution)/shard_map/ppermute | solution.py:375
  41.6 0.1 join.3
  41.7 0.4 collective-permute-start.9
  42.0 6.7 %collective-permute-done.9.refs_3_ = bf16[64,896]{1,0:T(8,128)(2,1)S(1)} collective-permute-done((bf16[64,896]{1,0:T(8,128)(2,1)S(1)}, bf16[64,896]{1,0:T(8,128)(2,1)S(1)}, u32[]{:S(2)}, u32[]{:S(2)}) %collective-permute-start.9) | collective-permute-done | bytes 114720 | tf_op jit(solution)/shard_map/ppermute | solution.py:375
  48.7 0.0 collective-permute-done.7.refs_1_
  48.7 0.9 %finish.1 = (f32[1,2048]{1,0:T(1,128)}, f32[64,2048]{1,0:T(8,128)}) custom-call(s32[1,2048]{1,0:T(1,128)S(1)} %bitcast.5, f32[72,1280]{1,0:T(8,128)S(1)} %get-tuple-element.32.refs_0_, bf16[64,1280]{1,0:T(8,128)(2,1)S(1)} %collective-permute-done.7.refs_1_, f32[72,768]{1,0:T(8,128)S(1)} %get-tuple-element.36.refs_2_, ...), custom_call_target="tpu_custom_call" | custom-call | tf_op jit(solution)/shard_map/finish/pallas_call | solution.py:347
Async XLA Ops:
  1.3 0.7 %copy-start.1 = (s32[2048]{0:T(1024)S(1)}, s32[2048]{0:T(1024)}, u32[]{:S(2)}) copy-start(s32[2048]{0:T(1024)} %param.5) | copy-start | bytes 24580
  3.1 14.1 %collective-permute-start.1 = (bf16[528,256]{1,0:T(8,128)(2,1)S(1)}, bf16[528,256]{1,0:T(8,128)(2,1)S(1)}, u32[]{:S(2)}, u32[]{:S(2)}) collective-permute-start(bf16[528,256]{1,0:T(8,128)(2,1)S(1)} %get-tuple-element.22.message_ref), channel_id=1, source_target_pairs={{0,248},{1,249},{2,250},{3,251},{4,12},{5,13},{6,14},{7,15},{8,0},... | collective-permute-start | bytes 811016 | tf_op jit(solution)/shard_map/ppermute | solution.py:375
  12.1 9.6 %collective-permute-start = (bf16[528,256]{1,0:T(8,128)(2,1)S(1)}, bf16[528,256]{1,0:T(8,128)(2,1)S(1)}, u32[]{:S(2)}, u32[]{:S(2)}) collective-permute-start(bf16[528,256]{1,0:T(8,128)(2,1)S(1)} %get-tuple-element.22.message_ref), channel_id=1, source_target_pairs={{0,6},{1,7},{2,4},{3,5},{4,2},{5,3},{6,0},{7,1},{8,14},{9,15},{10,... | collective-permute-start | bytes 811016 | tf_op jit(solution)/shard_map/ppermute | solution.py:375
  12.1 12.3 %collective-permute-start.2 = (bf16[528,256]{1,0:T(8,128)(2,1)S(1)}, bf16[528,256]{1,0:T(8,128)(2,1)S(1)}, u32[]{:S(2)}, u32[]{:S(2)}) collective-permute-start(bf16[528,256]{1,0:T(8,128)(2,1)S(1)} %get-tuple-element.22.message_ref), channel_id=1, source_target_pairs={{0,8},{1,9},{2,10},{3,11},{4,252},{5,253},{6,254},{7,255},{8,16},{... | collective-permute-start | bytes 811016 | tf_op jit(solution)/shard_map/ppermute | solution.py:375
  12.1 1.2 %copy-start = (bf16[2048,256]{1,0:T(8,128)(2,1)S(1)}, bf16[2048,256]{1,0:T(8,128)(2,1)}, u32[]{:S(2)}) copy-start(bf16[2048,256]{1,0:T(8,128)(2,1)} %query_ref.9) | copy-start | bytes 3145732
  17.2 11.9 %collective-permute-start.3 = (bf16[528,256]{1,0:T(8,128)(2,1)S(1)}, bf16[528,256]{1,0:T(8,128)(2,1)S(1)}, u32[]{:S(2)}, u32[]{:S(2)}) collective-permute-start(bf16[528,256]{1,0:T(8,128)(2,1)S(1)} %collective-permute-done.1.refs_1_), channel_id=1, source_target_pairs={{0,254},{1,255},{2,252},{3,253},{4,10},{5,11},{6,8},{7,9},{8,6},{9... | collective-permute-start | bytes 811016 | tf_op jit(solution)/shard_map/ppermute | solution.py:375
  21.6 12.0 %collective-permute-start.4 = (bf16[528,256]{1,0:T(8,128)(2,1)S(1)}, bf16[528,256]{1,0:T(8,128)(2,1)S(1)}, u32[]{:S(2)}, u32[]{:S(2)}) collective-permute-start(bf16[528,256]{1,0:T(8,128)(2,1)S(1)} %collective-permute-done.1.refs_1_), channel_id=1, source_target_pairs={{0,6},{1,7},{2,4},{3,5},{4,2},{5,3},{6,0},{7,1},{8,14},{9,15},{10,... | collective-permute-start | bytes 811016 | tf_op jit(solution)/shard_map/ppermute | solution.py:375
  21.6 12.0 %collective-permute-start.5 = (bf16[528,256]{1,0:T(8,128)(2,1)S(1)}, bf16[528,256]{1,0:T(8,128)(2,1)S(1)}, u32[]{:S(2)}, u32[]{:S(2)}) collective-permute-start(bf16[528,256]{1,0:T(8,128)(2,1)S(1)} %collective-permute-done.refs_0_), channel_id=1, source_target_pairs={{0,248},{1,249},{2,250},{3,251},{4,12},{5,13},{6,14},{7,15},{8,0},... | collective-permute-start | bytes 811016 | tf_op jit(solution)/shard_map/ppermute | solution.py:375
  35.5 4.7 %collective-permute-start.6 = (f32[136,1280]{1,0:T(8,128)S(1)}, f32[136,1280]{1,0:T(8,128)S(1)}, u32[]{:S(2)}, u32[]{:S(2)}) collective-permute-start(f32[136,1280]{1,0:T(8,128)S(1)} %get-tuple-element.31), channel_id=1, source_target_pairs={{0,1},{1,0},{2,3},{3,2},{4,5},{5,4},{6,7},{7,6},{8,9},{9,8},{10,11... | collective-permute-start | bytes 2088968 | tf_op jit(solution)/shard_map/ppermute | solution.py:375
  39.5 2.1 %collective-permute-start.8 = (f32[136,768]{1,0:T(8,128)S(1)}, f32[136,768]{1,0:T(8,128)S(1)}, u32[]{:S(2)}, u32[]{:S(2)}) collective-permute-start(f32[136,768]{1,0:T(8,128)S(1)} %get-tuple-element.35), channel_id=1, source_target_pairs={{0,1},{1,0},{2,3},{3,2},{4,5},{5,4},{6,7},{7,6},{8,9},{9,8},{10,11... | collective-permute-start | bytes 1253384 | tf_op jit(solution)/shard_map/ppermute | solution.py:375
  40.3 8.4 %collective-permute-start.7 = (bf16[64,1280]{1,0:T(8,128)(2,1)S(1)}, bf16[64,1280]{1,0:T(8,128)(2,1)S(1)}, u32[]{:S(2)}, u32[]{:S(2)}) collective-permute-start(bf16[64,1280]{1,0:T(8,128)(2,1)S(1)} %get-tuple-element.33), channel_id=1, source_target_pairs={{0,2},{1,3},{2,0},{3,1},{4,6},{5,7},{6,4},{7,5},{8,10},{9,11},{10,... | collective-permute-start | bytes 491528 | tf_op jit(solution)/shard_map/ppermute | solution.py:375
  41.7 7.0 %collective-permute-start.9 = (bf16[64,896]{1,0:T(8,128)(2,1)S(1)}, bf16[64,896]{1,0:T(8,128)(2,1)S(1)}, u32[]{:S(2)}, u32[]{:S(2)}) collective-permute-start(bf16[64,896]{1,0:T(8,128)(2,1)S(1)} %get-tuple-element.37), channel_id=1, source_target_pairs={{0,2},{1,3},{2,0},{3,1},{4,6},{5,7},{6,4},{7,5},{8,10},{9,11},{10,... | collective-permute-start | bytes 344072 | tf_op jit(solution)/shard_map/ppermute | solution.py:375

commit v2 on v1

--- a/solution.py
+++ b/solution.py
@@ -38,6 +38,12 @@
     middle = rest.astype(BF16)
     low = (rest - middle.astype(F32)).astype(BF16)
     return high, middle, low
+
+
+def as_rows(line):
+    parts = [part.astype(F32) for part in split3(line)]
+    parts.append(jnp.zeros((EXTRA - 3, line.shape[1]), F32))
+    return jnp.concatenate(parts, 0).astype(BF16)
 
 
 def own_turn():
@@ -209,9 +215,10 @@
         for half in range(2):
             first, second = quarter[2 * half], quarter[2 * half + 1]
             keep_ref[PART * half : PART * (half + 1), there] = jnp.where(core == 0, first, second)
-            send_ref[PART * half : PART * (half + 1), there] = jnp.where(core == 0, second, first)
+            given = jnp.where(core == 0, second, first).astype(BF16)
+            send_ref[PART * half : PART * (half + 1), there] = given
         keep_ref[2 * PART :, there] = total
-        send_ref[2 * PART :, there] = total
+        send_ref[2 * PART :, there] = as_rows(total[:1])
 
 
 def cost(shares):
@@ -268,13 +275,14 @@
 
 def last(query, bias, sums, messages, begin, size):
     shares = len(messages)
-    shape = jax.ShapeDtypeStruct((2 * PART + 8, size), F32)
+    kept = jax.ShapeDtypeStruct((2 * PART + 8, size), F32)
+    given = jax.ShapeDtypeStruct((2 * PART + EXTRA, size), BF16)
     scratch = line_up(shares) + [((size, GRANULE), F32), ((size, WIDTH), F32)]
     return pl.pallas_call(
         functools.partial(last_body, shares, begin, size),
         in_specs=[WHOLE] * (4 + shares),
         out_specs=(WHOLE, WHOLE),
-        out_shape=(shape, shape),
+        out_shape=(kept, given),
         scratch_shapes=[pltpu.VMEM(*spec) for spec in scratch],
         compiler_params=PARAMS,
         cost_estimate=cost(len(messages) * size / SLOTS),
@@ -286,9 +294,10 @@
     *before, sum_ref, message_ref = refs
     size = keep_ref.shape[1]
     chip = lax.axis_index("rep") // 2
-    both = keep_ref[...] + came_ref[...]
-    low, high = both[:PART], both[PART : 2 * PART]
-    total = both[2 * PART :]
+    both = keep_ref[: 2 * PART, :] + came_ref[: 2 * PART, :].astype(F32)
+    low, high = both[:PART], both[PART:]
+    extra = came_ref[2 * PART :, :].astype(F32)
+    total = keep_ref[2 * PART :, :] + (extra[0:1] + extra[1:2] + extra[2:3])
     sum_ref[:PART, :] = jnp.where(chip == 0, low, high)
     sum_ref[PART:, :] = total
     message_ref[:, :size] = jnp.where(chip == 0, high, low).astype(BF16)

time: 49.8 us -> 48.4 us (0.972)
  the two profiles are of different devices: /device:TPU:1 before, /device:TPU:4 now
where the time goes in v2:
time: 48.4 us; the launch traced here: 47.5 us
  starting transfers between devices  16.3 us (34%)
  waiting for transfers between devices  15.7 us (32%)
  Pallas kernels  12.3 us (25%)
  local copies, waits for them, and re-layouts  1.91 us (4%)
  between operations  1.36 us (3%)
    ppermute x10, starting transfers between devices, send(): return lax.ppermute(value, ('blk', 'rep'), route(blocks, reps, move))  16.3 us
    ppermute x10, waiting for transfers between devices, send(): return lax.ppermute(value, ('blk', 'rep'), route(blocks, reps, move))  15.7 us
    pallas_call x2, Pallas kernels, middle(): pl.pallas_call(functools.partial(middle_body, shares), in_specs=[WHOLE] *...  3.76 us
    pallas_call x2, Pallas kernels, last(): pl.pallas_call(functools.partial(last_body, shares, begin, size), in_spec...  3.38 us
    pallas_call x1, Pallas kernels, first(): pl.pallas_call(first_body, grid=(SLOTS // TILE,), in_specs=[QUERY, MESSAG...  2.88 us
    unnamed x4, local copies, waits for them, and re-layouts  1.91 us
    pallas_call x1, Pallas kernels, pack(): pl.pallas_call(pack_body, in_specs=[pl.BlockSpec(memory_space=pl.ANY)] *...  1.15 us
  transfers between devices with their start and end apart: 10, of which 5 were waited for; matrix products, arithmetic and copies ran while one was open for 0% of the time, Pallas kernels for 17%

profile of v2, /device:TPU:4, one launch (start us, length us, event | category | flops | bytes accessed | tf_op | source)
XLA Modules:
  0.0 47.5 jit_solution(16761825315204962133)
XLA Ops:
  1.3 0.0 copy-start.1
  1.3 0.7 %copy-done.1 = s32[2048]{0:T(1024)S(1)} copy-done((s32[2048]{0:T(1024)S(1)}, s32[2048]{0:T(1024)}, u32[]{:S(2)}) %copy-start.1) | copy-done | bytes 8216
  2.0 1.2 %pack.1 = (bf16[528,256]{1,0:T(8,128)(2,1)S(1)}, s32[16,128]{1,0:T(8,128)S(1)}) custom-call(s32[1]{0:T(128)S(6)} %copy.13.counts_ref, bf16[2048,256]{1,0:T(8,128)(2,1)} %query_ref.9, s32[16,128]{1,0:T(8,128)S(1)} %bitcast.4), custom_call_target="tpu_custom_call" | custom-call | tf_op jit(solution)/shard_map/pack/pallas_call | solution.py:91
  3.1 2.0 %collective-permute-start.1 = (bf16[528,256]{1,0:T(8,128)(2,1)S(1)}, bf16[528,256]{1,0:T(8,128)(2,1)S(1)}, u32[]{:S(2)}, u32[]{:S(2)}) collective-permute-start(bf16[528,256]{1,0:T(8,128)(2,1)S(1)} %get-tuple-element.22.message_ref), channel_id=1, source_target_pairs={{0,248},{1,249},{2,250},{3,251},{4,12},{5,13},{6,14},{7,15},{8,0},... | collective-permute-start | bytes 811016 | tf_op jit(solution)/shard_map/ppermute | solution.py:384
  5.1 6.9 %collective-permute-start = (bf16[528,256]{1,0:T(8,128)(2,1)S(1)}, bf16[528,256]{1,0:T(8,128)(2,1)S(1)}, u32[]{:S(2)}, u32[]{:S(2)}) collective-permute-start(bf16[528,256]{1,0:T(8,128)(2,1)S(1)} %get-tuple-element.22.message_ref), channel_id=1, source_target_pairs={{0,6},{1,7},{2,4},{3,5},{4,2},{5,3},{6,0},{7,1},{8,14},{9,15},{10,... | collective-permute-start | bytes 811016 | tf_op jit(solution)/shard_map/ppermute | solution.py:384
  12.1 1.0 %collective-permute-start.2 = (bf16[528,256]{1,0:T(8,128)(2,1)S(1)}, bf16[528,256]{1,0:T(8,128)(2,1)S(1)}, u32[]{:S(2)}, u32[]{:S(2)}) collective-permute-start(bf16[528,256]{1,0:T(8,128)(2,1)S(1)} %get-tuple-element.22.message_ref), channel_id=1, source_target_pairs={{0,8},{1,9},{2,10},{3,11},{4,252},{5,253},{6,254},{7,255},{8,16},{... | collective-permute-start | bytes 811016 | tf_op jit(solution)/shard_map/ppermute | solution.py:384
  13.1 0.0 copy-start
  13.1 1.2 %copy-done = bf16[2048,256]{1,0:T(8,128)(2,1)S(1)} copy-done((bf16[2048,256]{1,0:T(8,128)(2,1)S(1)}, bf16[2048,256]{1,0:T(8,128)(2,1)}, u32[]{:S(2)}) %copy-start) | copy-done | bytes 1048600
  14.3 2.9 %first.1 = (f32[2048,128]{1,0:T(8,128)S(1)}, f32[2048,256]{1,0:T(8,128)S(1)}, f32[2048,128]{1,0:T(8,128)S(1)}) custom-call(bf16[2048,256]{1,0:T(8,128)(2,1)S(1)} %copy-done, bf16[528,256]{1,0:T(8,128)(2,1)S(1)} %get-tuple-element.22.message_ref), custom_call_target="tpu_custom_call" | custom-call | flops 1073741824 | bytes 6291456 | tf_op jit(solution)/shard_map/first/pallas_call | solution.py:245
  17.2 0.8 %collective-permute-done.1.refs_1_ = bf16[528,256]{1,0:T(8,128)(2,1)S(1)} collective-permute-done((bf16[528,256]{1,0:T(8,128)(2,1)S(1)}, bf16[528,256]{1,0:T(8,128)(2,1)S(1)}, u32[]{:S(2)}, u32[]{:S(2)}) %collective-permute-start.1) | collective-permute-done | bytes 270368 | tf_op jit(solution)/shard_map/ppermute | solution.py:384
  18.0 0.0 collective-permute-start.3
  18.0 3.2 %collective-permute-start.4 = (bf16[528,256]{1,0:T(8,128)(2,1)S(1)}, bf16[528,256]{1,0:T(8,128)(2,1)S(1)}, u32[]{:S(2)}, u32[]{:S(2)}) collective-permute-start(bf16[528,256]{1,0:T(8,128)(2,1)S(1)} %collective-permute-done.1.refs_1_), channel_id=1, source_target_pairs={{0,6},{1,7},{2,4},{3,5},{4,2},{5,3},{6,0},{7,1},{8,14},{9,15},{10,... | collective-permute-start | bytes 811016 | tf_op jit(solution)/shard_map/ppermute | solution.py:384
  21.2 0.0 collective-permute-done.refs_0_
  21.2 0.3 collective-permute-start.5
  21.5 0.0 collective-permute-done.2.refs_2_
  21.5 1.8 %middle.2 = (f32[2048,128]{1,0:T(8,128)S(1)}, f32[2048,256]{1,0:T(8,128)S(1)}) custom-call(bf16[2048,256]{1,0:T(8,128)(2,1)S(1)} %copy-done, f32[2048,128]{1,0:T(8,128)S(1)} %get-tuple-element.23.bias_ref, f32[2048,128]{1,0:T(8,128)S(1)} %get-tuple-element.24.total_in, ...), custom_call_target="tpu_custom_call", output_to_operand_aliasing={{0}: (2, {}), {1}: (3, {})} | custom-call | flops 3221225472 | bytes 6291456 | tf_op jit(solution)/shard_map/middle/pallas_call | solution.py:263
  23.3 5.0 %collective-permute-done.3.refs_0_ = bf16[528,256]{1,0:T(8,128)(2,1)S(1)} collective-permute-done((bf16[528,256]{1,0:T(8,128)(2,1)S(1)}, bf16[528,256]{1,0:T(8,128)(2,1)S(1)}, u32[]{:S(2)}, u32[]{:S(2)}) %collective-permute-start.3) | collective-permute-done | bytes 270368 | tf_op jit(solution)/shard_map/ppermute | solution.py:384
  28.3 1.9 %middle.3 = (f32[2048,128]{1,0:T(8,128)S(1)}, f32[2048,256]{1,0:T(8,128)S(1)}) custom-call(bf16[2048,256]{1,0:T(8,128)(2,1)S(1)} %copy-done, f32[2048,128]{1,0:T(8,128)S(1)} %get-tuple-element.23.bias_ref, f32[2048,128]{1,0:T(8,128)S(1)} %get-tuple-element.26.total_in, ...), custom_call_target="tpu_custom_call", output_to_operand_aliasing={{0}: (2, {}), {1}: (3, {})} | custom-call | flops 1073741824 | bytes 6291456 | tf_op jit(solution)/shard_map/middle/pallas_call | solution.py:263
  30.3 2.1 %collective-permute-done.4.refs_0_ = bf16[528,256]{1,0:T(8,128)(2,1)S(1)} collective-permute-done((bf16[528,256]{1,0:T(8,128)(2,1)S(1)}, bf16[528,256]{1,0:T(8,128)(2,1)S(1)}, u32[]{:S(2)}, u32[]{:S(2)}) %collective-permute-start.4) | collective-permute-done | bytes 270368 | tf_op jit(solution)/shard_map/ppermute | solution.py:384
  32.3 1.4 %collective-permute-done.5.refs_1_ = bf16[528,256]{1,0:T(8,128)(2,1)S(1)} collective-permute-done((bf16[528,256]{1,0:T(8,128)(2,1)S(1)}, bf16[528,256]{1,0:T(8,128)(2,1)S(1)}, u32[]{:S(2)}, u32[]{:S(2)}) %collective-permute-start.5) | collective-permute-done | bytes 270368 | tf_op jit(solution)/shard_map/ppermute | solution.py:384
  33.7 1.9 %last.2 = (f32[136,1280]{1,0:T(8,128)S(1)}, bf16[144,1280]{1,0:T(8,128)(2,1)S(1)}) custom-call(bf16[2048,256]{1,0:T(8,128)(2,1)S(1)} %copy-done, f32[2048,128]{1,0:T(8,128)S(1)} %get-tuple-element.23.bias_ref, f32[2048,128]{1,0:T(8,128)S(1)} %get-tuple-element.28.total_in, f32[2048,256]{1,0:T(8,128)S(1)} %get-tuple-element.29.weighted_in, ...), custom_call_target="tpu_custom_call" | custom-call | flops 1342177280 | bytes 6291456 | tf_op jit(solution)/shard_map/last/pallas_call | solution.py:281
  35.7 0.1 collective-permute-start.6
  35.8 1.4 %last.3 = (f32[136,768]{1,0:T(8,128)S(1)}, bf16[144,768]{1,0:T(8,128)(2,1)S(1)}) custom-call(bf16[2048,256]{1,0:T(8,128)(2,1)S(1)} %copy-done, f32[2048,128]{1,0:T(8,128)S(1)} %get-tuple-element.23.bias_ref, f32[2048,128]{1,0:T(8,128)S(1)} %get-tuple-element.28.total_in, f32[2048,256]{1,0:T(8,128)S(1)} %get-tuple-element.29.weighted_in, ...), custom_call_target="tpu_custom_call" | custom-call | flops 805306368 | bytes 6291456 | tf_op jit(solution)/shard_map/last/pallas_call | solution.py:281
  37.2 0.6 %collective-permute-start.8 = (bf16[144,768]{1,0:T(8,128)(2,1)S(1)}, bf16[144,768]{1,0:T(8,128)(2,1)S(1)}, u32[]{:S(2)}, u32[]{:S(2)}) collective-permute-start(bf16[144,768]{1,0:T(8,128)(2,1)S(1)} %get-tuple-element.35), channel_id=1, source_target_pairs={{0,1},{1,0},{2,3},{3,2},{4,5},{5,4},{6,7},{7,6},{8,9},{9,8},{10,11... | collective-permute-start | bytes 663560 | tf_op jit(solution)/shard_map/ppermute | solution.py:384
  37.8 0.0 collective-permute-done.6.came_ref
  37.8 0.1 join.2
  37.9 1.0 %collective-permute-start.7 = (bf16[64,1280]{1,0:T(8,128)(2,1)S(1)}, bf16[64,1280]{1,0:T(8,128)(2,1)S(1)}, u32[]{:S(2)}, u32[]{:S(2)}) collective-permute-start(bf16[64,1280]{1,0:T(8,128)(2,1)S(1)} %get-tuple-element.33), channel_id=1, source_target_pairs={{0,2},{1,3},{2,0},{3,1},{4,6},{5,7},{6,4},{7,5},{8,10},{9,11},{10,... | collective-permute-start | bytes 491528 | tf_op jit(solution)/shard_map/ppermute | solution.py:384
  38.9 0.0 collective-permute-done.8.came_ref
  38.9 0.1 join.3
  39.0 1.2 %collective-permute-start.9 = (bf16[64,896]{1,0:T(8,128)(2,1)S(1)}, bf16[64,896]{1,0:T(8,128)(2,1)S(1)}, u32[]{:S(2)}, u32[]{:S(2)}) collective-permute-start(bf16[64,896]{1,0:T(8,128)(2,1)S(1)} %get-tuple-element.37), channel_id=1, source_target_pairs={{0,2},{1,3},{2,0},{3,1},{4,6},{5,7},{6,4},{7,5},{8,10},{9,11},{10,... | collective-permute-start | bytes 344072 | tf_op jit(solution)/shard_map/ppermute | solution.py:384
  40.2 6.4 %collective-permute-done.9.refs_3_ = bf16[64,896]{1,0:T(8,128)(2,1)S(1)} collective-permute-done((bf16[64,896]{1,0:T(8,128)(2,1)S(1)}, bf16[64,896]{1,0:T(8,128)(2,1)S(1)}, u32[]{:S(2)}, u32[]{:S(2)}) %collective-permute-start.9) | collective-permute-done | bytes 114720 | tf_op jit(solution)/shard_map/ppermute | solution.py:384
  46.6 0.0 collective-permute-done.7.refs_1_
  46.6 0.9 %finish.1 = (f32[1,2048]{1,0:T(1,128)}, f32[64,2048]{1,0:T(8,128)}) custom-call(s32[1,2048]{1,0:T(1,128)S(1)} %bitcast.5, f32[72,1280]{1,0:T(8,128)S(1)} %get-tuple-element.32.refs_0_, bf16[64,1280]{1,0:T(8,128)(2,1)S(1)} %collective-permute-done.7.refs_1_, f32[72,768]{1,0:T(8,128)S(1)} %get-tuple-element.36.refs_2_, ...), custom_call_target="tpu_custom_call" | custom-call | tf_op jit(solution)/shard_map/finish/pallas_call | solution.py:356
Async XLA Ops:
  1.3 0.7 %copy-start.1 = (s32[2048]{0:T(1024)S(1)}, s32[2048]{0:T(1024)}, u32[]{:S(2)}) copy-start(s32[2048]{0:T(1024)} %param.5) | copy-start | bytes 24580
  3.1 14.9 %collective-permute-start.1 = (bf16[528,256]{1,0:T(8,128)(2,1)S(1)}, bf16[528,256]{1,0:T(8,128)(2,1)S(1)}, u32[]{:S(2)}, u32[]{:S(2)}) collective-permute-start(bf16[528,256]{1,0:T(8,128)(2,1)S(1)} %get-tuple-element.22.message_ref), channel_id=1, source_target_pairs={{0,248},{1,249},{2,250},{3,251},{4,12},{5,13},{6,14},{7,15},{8,0},... | collective-permute-start | bytes 811016 | tf_op jit(solution)/shard_map/ppermute | solution.py:384
  5.1 16.1 %collective-permute-start = (bf16[528,256]{1,0:T(8,128)(2,1)S(1)}, bf16[528,256]{1,0:T(8,128)(2,1)S(1)}, u32[]{:S(2)}, u32[]{:S(2)}) collective-permute-start(bf16[528,256]{1,0:T(8,128)(2,1)S(1)} %get-tuple-element.22.message_ref), channel_id=1, source_target_pairs={{0,6},{1,7},{2,4},{3,5},{4,2},{5,3},{6,0},{7,1},{8,14},{9,15},{10,... | collective-permute-start | bytes 811016 | tf_op jit(solution)/shard_map/ppermute | solution.py:384
  12.1 9.4 %collective-permute-start.2 = (bf16[528,256]{1,0:T(8,128)(2,1)S(1)}, bf16[528,256]{1,0:T(8,128)(2,1)S(1)}, u32[]{:S(2)}, u32[]{:S(2)}) collective-permute-start(bf16[528,256]{1,0:T(8,128)(2,1)S(1)} %get-tuple-element.22.message_ref), channel_id=1, source_target_pairs={{0,8},{1,9},{2,10},{3,11},{4,252},{5,253},{6,254},{7,255},{8,16},{... | collective-permute-start | bytes 811016 | tf_op jit(solution)/shard_map/ppermute | solution.py:384
  13.1 1.2 %copy-start = (bf16[2048,256]{1,0:T(8,128)(2,1)S(1)}, bf16[2048,256]{1,0:T(8,128)(2,1)}, u32[]{:S(2)}) copy-start(bf16[2048,256]{1,0:T(8,128)(2,1)} %query_ref.9) | copy-start | bytes 3145732
  18.0 10.3 %collective-permute-start.3 = (bf16[528,256]{1,0:T(8,128)(2,1)S(1)}, bf16[528,256]{1,0:T(8,128)(2,1)S(1)}, u32[]{:S(2)}, u32[]{:S(2)}) collective-permute-start(bf16[528,256]{1,0:T(8,128)(2,1)S(1)} %collective-permute-done.1.refs_1_), channel_id=1, source_target_pairs={{0,254},{1,255},{2,252},{3,253},{4,10},{5,11},{6,8},{7,9},{8,6},{9... | collective-permute-start | bytes 811016 | tf_op jit(solution)/shard_map/ppermute | solution.py:384
  18.0 14.3 %collective-permute-start.4 = (bf16[528,256]{1,0:T(8,128)(2,1)S(1)}, bf16[528,256]{1,0:T(8,128)(2,1)S(1)}, u32[]{:S(2)}, u32[]{:S(2)}) collective-permute-start(bf16[528,256]{1,0:T(8,128)(2,1)S(1)} %collective-permute-done.1.refs_1_), channel_id=1, source_target_pairs={{0,6},{1,7},{2,4},{3,5},{4,2},{5,3},{6,0},{7,1},{8,14},{9,15},{10,... | collective-permute-start | bytes 811016 | tf_op jit(solution)/shard_map/ppermute | solution.py:384
  21.2 12.5 %collective-permute-start.5 = (bf16[528,256]{1,0:T(8,128)(2,1)S(1)}, bf16[528,256]{1,0:T(8,128)(2,1)S(1)}, u32[]{:S(2)}, u32[]{:S(2)}) collective-permute-start(bf16[528,256]{1,0:T(8,128)(2,1)S(1)} %collective-permute-done.refs_0_), channel_id=1, source_target_pairs={{0,248},{1,249},{2,250},{3,251},{4,12},{5,13},{6,14},{7,15},{8,0},... | collective-permute-start | bytes 811016 | tf_op jit(solution)/shard_map/ppermute | solution.py:384
  35.7 2.1 %collective-permute-start.6 = (bf16[144,1280]{1,0:T(8,128)(2,1)S(1)}, bf16[144,1280]{1,0:T(8,128)(2,1)S(1)}, u32[]{:S(2)}, u32[]{:S(2)}) collective-permute-start(bf16[144,1280]{1,0:T(8,128)(2,1)S(1)} %get-tuple-element.31), channel_id=1, source_target_pairs={{0,1},{1,0},{2,3},{3,2},{4,5},{5,4},{6,7},{7,6},{8,9},{9,8},{10,11... | collective-permute-start | bytes 1105928 | tf_op jit(solution)/shard_map/ppermute | solution.py:384
  37.2 1.7 %collective-permute-start.8 = (bf16[144,768]{1,0:T(8,128)(2,1)S(1)}, bf16[144,768]{1,0:T(8,128)(2,1)S(1)}, u32[]{:S(2)}, u32[]{:S(2)}) collective-permute-start(bf16[144,768]{1,0:T(8,128)(2,1)S(1)} %get-tuple-element.35), channel_id=1, source_target_pairs={{0,1},{1,0},{2,3},{3,2},{4,5},{5,4},{6,7},{7,6},{8,9},{9,8},{10,11... | collective-permute-start | bytes 663560 | tf_op jit(solution)/shard_map/ppermute | solution.py:384
  37.9 8.7 %collective-permute-start.7 = (bf16[64,1280]{1,0:T(8,128)(2,1)S(1)}, bf16[64,1280]{1,0:T(8,128)(2,1)S(1)}, u32[]{:S(2)}, u32[]{:S(2)}) collective-permute-start(bf16[64,1280]{1,0:T(8,128)(2,1)S(1)} %get-tuple-element.33), channel_id=1, source_target_pairs={{0,2},{1,3},{2,0},{3,1},{4,6},{5,7},{6,4},{7,5},{8,10},{9,11},{10,... | collective-permute-start | bytes 491528 | tf_op jit(solution)/shard_map/ppermute | solution.py:384
  39.0 7.6 %collective-permute-start.9 = (bf16[64,896]{1,0:T(8,128)(2,1)S(1)}, bf16[64,896]{1,0:T(8,128)(2,1)S(1)}, u32[]{:S(2)}, u32[]{:S(2)}) collective-permute-start(bf16[64,896]{1,0:T(8,128)(2,1)S(1)} %get-tuple-element.37), channel_id=1, source_target_pairs={{0,2},{1,3},{2,0},{3,1},{4,6},{5,7},{6,4},{7,5},{8,10},{9,11},{10,... | collective-permute-start | bytes 344072 | tf_op jit(solution)/shard_map/ppermute | solution.py:384
